TPU v7x, 512 devices: a whole 4x4x16 slice. The times are simulated.
512 devices in a mesh: dp: 64 (over z, x), cent: 8 (over y, core).
Axes of the slice: x: 4, y: 4, z: 16, core: 2. Of those that a mesh axis runs over, the one named last changes fastest.
Arguments:
- embeddings: float32 [98304, 1024], P(('dp', 'cent')), may hold values from -128 to 128
- centroids: float32 [4096, 1024], P(('dp', 'cent')), may hold values from -6 to 6
Outputs:
- updated: float32 [4096, 1024], P(('dp', 'cent'))
- entropy: float32 [98304], P(('dp', 'cent'))
All inputs are finite; a program needn't handle non-finite values.
Results may differ from a plain program's by a relative error of at most 0.024.
Values may be sent and summed in bfloat16 or wider, within the bound.
A program may use at most 64 MiB of HBM per device.

v0:
```python
import jax
import jax.numpy as jnp
from jax import lax
from jax.sharding import PartitionSpec as P

softness_level = 32.0
prior_mass = 4.0


def row_stats(score):
    top = lax.pmax(jnp.max(score, axis=1), "cent")
    shifted = score - top[:, None]
    weight = jnp.exp(shifted)
    total, spread = lax.psum((jnp.sum(weight, axis=1), jnp.sum(weight * shifted, axis=1)), "cent")
    return (weight, total, spread)


def on_device(embeddings, centroids):
    shard_rows = embeddings.shape[0]
    per_device = centroids.shape[0]
    rows_b = lax.all_gather(embeddings.astype(jnp.bfloat16), "cent", axis=0, tiled=True)
    row_squared_norm = jnp.einsum("rd,rd->r", rows_b, rows_b, preferred_element_type=jnp.float32)

    def score_piece(piece):
        inner_products = jnp.einsum("rd,kd->rk", rows_b, piece, preferred_element_type=jnp.float32)
        centroid_squared_norm = jnp.einsum(
            "kd,kd->k", piece, piece, preferred_element_type=jnp.float32
        )
        return -(
            row_squared_norm[:, None] - 2.0 * inner_products + centroid_squared_norm[None, :]
        ) / (2.0 * softness_level)

    previous = lax.all_gather(centroids, "dp", axis=0, tiled=True)
    first_score = score_piece(previous.astype(jnp.bfloat16))
    weight, total, unused = row_stats(first_score)
    resp = (weight / total[:, None]).astype(jnp.bfloat16)
    sums = jnp.einsum("rk,rd->kd", resp, rows_b, preferred_element_type=jnp.float32)
    counts = jnp.sum(resp, axis=0, dtype=jnp.float32)
    sums, counts = lax.psum((sums, counts), "dp")
    renewed = (sums + prior_mass * previous) / (counts + prior_mass)[:, None]
    second_score = score_piece(renewed.astype(jnp.bfloat16))
    updated = lax.dynamic_slice_in_dim(renewed, lax.axis_index("dp") * per_device, per_device, 0)
    unused_weight, total_two, spread_two = row_stats(second_score)
    entropy_group = jnp.log(total_two) - spread_two / total_two
    entropy = lax.dynamic_slice_in_dim(
        entropy_group, lax.axis_index("cent") * shard_rows, shard_rows, 0
    )
    return (updated, entropy)


def solution(mesh):
    in_specs = (P(("dp", "cent"), None), P(("dp", "cent"), None))
    out_specs = (P(("dp", "cent"), None), P(("dp", "cent")))
    return jax.shard_map(
        on_device, mesh=mesh, in_specs=in_specs, out_specs=out_specs, check_vma=False
    )
```

profile of v0, /device:TPU:1, one launch (start us, length us, event | category | flops | bytes accessed | tf_op | source)
XLA Modules:
  0.0 554.2 jit_solution(14414624586229373610)
XLA Ops:
  7.2 0.0 all-gather.5.cloned.1.call-start
  7.2 0.7 all-gather.5.cloned.1.call-update
  7.9 0.0 all-gather.3.cloned.1.call-start
  7.9 1.9 convert_element_type.15
  9.9 0.0 all-gather.3.cloned.1.call-update
  9.9 0.0 all-reduce.3.cloned.1.call-start
  10.0 138.4 %all-gather.5.cloned.1.call-done = f32[512,1024]{1,0:T(8,128)} async-done(((f32[8,1024]{1,0:T(8,128)}), f32[512,1024]{1,0:T(8,128)}) %all-gather.5.cloned.1.call-update) | async-done | bytes 2097168 | tf_op jit(solution)/shard_map/all_gather | solution.py:33
  148.4 1.8 fusion.12
  150.2 41.1 %all-gather.3.cloned.1.call-done = bf16[1536,1024]{1,0:T(8,128)(2,1)} async-done(((bf16[192,1024]{1,0:T(8,128)(2,1)}), bf16[1536,1024]{1,0:T(8,128)(2,1)}) %all-gather.3.cloned.1.call-update) | async-done | bytes 3145744 | tf_op jit(solution)/shard_map/all_gather | solution.py:21
  191.3 0.0 copy-start
  191.3 2.7 fusion
  194.0 0.0 copy-done
  194.0 3.9 fusion.15
  197.9 12.2 %pmax.14 = f32[1536]{0:T(1024)S(1)} all-reduce(f32[1536]{0:T(1024)S(1)} %get-tuple-element.10), channel_id=1, replica_groups=mesh['dp'=64,'cent'=8] {'cent'}, use_global_device_ids=true, to_apply=%region_1.0 | all-reduce | flops 1536 | bytes 12288 | tf_op jit(solution)/shard_map/pmax | solution.py:11
  210.2 0.5 fusion.10
  210.6 14.1 %psum.35 = f32[1536]{0:T(1024)S(1)} all-reduce(f32[1536]{0:T(1024)S(1)} %fusion.10), channel_id=1, replica_groups=mesh['dp'=64,'cent'=8] {'cent'}, use_global_device_ids=true, to_apply=%region_3.0 | all-reduce | flops 1536 | bytes 12288 | tf_op jit(solution)/shard_map/psum | solution.py:14
  224.7 0.0 copy-start.2
  224.7 0.6 convert_reduce_fusion
  225.4 1.2 copy-done.2
  226.6 3.2 fusion.17
  229.8 0.0 copy-start.1
  229.8 0.0 all-reduce.3.cloned.1.call-update
  229.8 116.5 %psum.37 = f32[512]{0:T(512)S(1)} all-reduce(f32[512]{0:T(512)S(1)} %get-tuple-element.8), channel_id=1, replica_groups=mesh['dp'=64,'cent'=8] {'dp'}, use_global_device_ids=true, to_apply=%region_6.0 | all-reduce | flops 512 | bytes 4096 | tf_op jit(solution)/shard_map/psum | solution.py:39
  346.3 151.5 %all-reduce.3.cloned.1.call-done = f32[512,1024]{1,0:T(8,128)} async-done(((f32[512,1024]{1,0:T(8,128)}), f32[512,1024]{1,0:T(8,128)}) %all-reduce.3.cloned.1.call-update) | async-done | bytes 2097168 | tf_op jit(solution)/shard_map/psum | solution.py:39
  497.8 0.0 copy-done.1
  497.8 0.0 copy-start.3
  497.8 2.2 fusion.11
  500.0 0.0 copy-start.4
  500.0 0.3 copy-done.3
  500.3 2.0 fusion.16
  502.3 0.0 copy-done.4
  502.3 21.9 %pmax.15 = f32[1536]{0:T(1024)S(1)} all-reduce(f32[1536]{0:T(1024)S(1)} %get-tuple-element.12), channel_id=1, replica_groups=mesh['dp'=64,'cent'=8] {'cent'}, use_global_device_ids=true, to_apply=%region_8.0 | all-reduce | flops 1536 | bytes 12288 | tf_op jit(solution)/shard_map/pmax | solution.py:11
  524.3 1.4 constant_dynamic-slice_fusion
  525.7 0.6 exponential_reduce_fusion
  526.3 20.7 %all-reduce = (f32[1536]{0:T(1024)S(1)}, f32[1536]{0:T(1024)S(1)}) all-reduce(f32[1536]{0:T(1024)S(1)} %get-tuple-element.3, f32[1536]{0:T(1024)S(1)} %get-tuple-element.2), channel_id=1, replica_groups=mesh['dp'=64,'cent'=8] {'cent'}, use_global_device_ids=true, to_apply=%region_12.0 | all-reduce | flops 3072 | bytes 24576 | tf_op jit(solution)/shard_map/psum | solution.py:14
  547.0 0.6 log_subtract_fusion
  (1 shorter events, 0.0 us)
Async XLA Ops:
  7.2 141.2 %all-gather.5.cloned.1.call-start = ((), (), s32[]{:S(2)}) async-start(), calls=%async_computation.1 | async-start | bytes 2129920 | tf_op jit(solution)/shard_map/all_gather | solution.py:33
  7.9 183.4 %all-gather.3.cloned.1.call-start = ((), (), s32[]{:S(2)}) async-start(), calls=%async_computation | async-start | bytes 3538944 | tf_op jit(solution)/shard_map/all_gather | solution.py:21
  9.9 487.9 %all-reduce.3.cloned.1.call-start = ((), (), s32[]{:S(2)}) async-start(), calls=%async_computation.2 | async-start | bytes 4194304 | tf_op jit(solution)/shard_map/psum | solution.py:39
  191.3 2.7 copy-start
  224.7 1.9 copy-start.2
  229.8 268.0 %copy-start.1 = (f32[512,1024]{1,0:T(8,128)S(1)}, f32[512,1024]{1,0:T(8,128)}, u32[]{:S(2)}) copy-start(f32[512,1024]{1,0:T(8,128)} %all-gather.5.cloned.1.call-done) | copy-start | bytes 6291460
  497.8 2.5 copy-start.3
  500.0 2.3 copy-start.4
Sparse Core Ops, SparseCore 0:
  10.9 137.3 all-gather.4
  150.5 40.7 all-gather.2
  229.9 267.8 all-reduce.2
where the time goes:
time: 556 us; the launch traced here: 554 us
  waiting for transfers between devices  332 us (60%)
  blocking collectives  185 us (33%)
  between operations  13.8 us (2%)
  other arithmetic  11.1 us (2%)
  matrix products  9.08 us (2%)
    psum x1, waiting for transfers between devices, on_device(): sums, counts = lax.psum((sums, counts), 'dp')  151 us
    all_gather x1, waiting for transfers between devices, on_device(): previous = lax.all_gather(centroids, 'dp', axis=0, tiled=True)  138 us
    psum x1, blocking collectives, on_device(): sums, counts = lax.psum((sums, counts), 'dp')  116 us
    all_gather x1, waiting for transfers between devices, on_device(): lax.all_gather(embeddings.astype(jnp.bfloat16), 'cent', axis=0, tiled=True)  41.1 us
    psum x2, blocking collectives, row_stats(): lax.psum((jnp.sum(weight, axis=1), jnp.sum(weight * shifted, axis=1)), 'c...  34.8 us
    pmax x2, blocking collectives, row_stats(): top = lax.pmax(jnp.max(score, axis=1), 'cent')  34.2 us
  transfers between devices with their start and end apart: 3, of which 3 were waited for; matrix products, arithmetic and copies ran while one was open for 1% of the time, Pallas kernels for 0%

commit v1 on v0

v1 whole, which is shorter than its diff:
```python
import jax
import jax.numpy as jnp
from jax import lax
from jax.experimental import pallas as pl
from jax.experimental.pallas import tpu as pltpu
from jax.sharding import PartitionSpec as P

MESH = pl.DeviceIdType.MESH
F32 = jnp.float32
BF16 = jnp.bfloat16

softness_level = 32.0
prior_mass = 4.0

D = 1024
NZ, NX, NY, NC = 16, 4, 4, 2
NCENT = NY * NC
ROWS = 192
GROUP = ROWS * NCENT
CHIP = ROWS * NC
OWN = 8
SLICE = OWN * NZ * NX
PARTS = 4
W = D // (2 * PARTS)
LANES = 128
TILES = GROUP // LANES
CHIP_TILES = CHIP // LANES
SCALE = 2.0 * softness_level


def place():
    dp = lax.axis_index("dp")
    cent = lax.axis_index("cent")
    z = dp // NX
    x = dp % NX
    y = cent // NC
    core = cent % NC
    return z, x, y, core, cent


def far_first(step):
    half = (step + 1) // 2
    return NZ // 2 + half * (1 - 2 * (step % 2))


def kernel(
    emb_hbm,
    cent_hbm,
    upd_out,
    ent_out,
    emb_v,
    cent_v,
    rows,
    first,
    second,
    operand,
    norm_part,
    norm,
    row_sq,
    acc,
    resp,
    stat_send,
    stat_recv,
    factor,
    stat2_send,
    stat2_recv,
    sums_f,
    sums_send,
    sums_recv,
    part_send,
    part_recv,
    count_send,
    count_recv,
    total_send,
    total_recv,
    load_sem,
    rows_send_sem,
    rows_recv_sem,
    gz_send,
    gz_recv,
    gx_send,
    gx_recv,
    st_send,
    st_recv,
    cx_send,
    cx_recv,
    cz_send,
    cz_recv,
    nx_send,
    nx_recv,
    nz_send,
    nz_recv,
    uz_send,
    uz_recv,
    ux_send,
    ux_recv,
    st2_send,
    st2_recv,
):
    z, x, y, core, cent = place()

    def at_zx(z_to, x_to):
        return {"dp": z_to * NX + x_to, "cent": cent}

    def at_cent(cent_to):
        return {"dp": z * NX + x, "cent": cent_to}

    def remote(src, dst, send, recv, device):
        return pltpu.make_async_remote_copy(
            src_ref=src, dst_ref=dst, send_sem=send, recv_sem=recv, device_id=device, device_id_type=MESH
        )

    def take(ref, sem):
        pltpu.make_async_copy(ref, ref, sem).wait()

    load_cent = pltpu.make_async_copy(cent_hbm, cent_v, load_sem.at[0])
    load_emb = pltpu.make_async_copy(emb_hbm, emb_v, load_sem.at[1])
    load_cent.start()
    load_emb.start()

    barrier = pltpu.get_barrier_semaphore()

    def greet_z(step, carry):
        pl.semaphore_signal(
            barrier, inc=1, device_id=at_zx((z + far_first(step)) % NZ, x), device_id_type=MESH
        )
        return carry

    lax.fori_loop(0, NZ - 1, greet_z, 0)
    for k in range(1, NCENT):
        pl.semaphore_signal(
            barrier, inc=1, device_id=at_cent((cent + k) % NCENT), device_id_type=MESH
        )
    for k in range(1, NX):
        pl.semaphore_signal(barrier, inc=1, device_id=at_zx(z, (x + k) % NX), device_id_type=MESH)

    load_cent.wait()
    for p in range(PARTS):
        left = cent_v[:, 2 * W * p : 2 * W * p + W]
        right = cent_v[:, 2 * W * p + W : 2 * W * (p + 1)]
        first[p, x, z] = jnp.concatenate([left, right], axis=0).astype(BF16)
    load_emb.wait()
    own_rows = pl.ds(pl.multiple_of(cent * ROWS, ROWS), ROWS)
    rows[own_rows, :] = emb_v[...].astype(BF16)

    pl.semaphore_wait(barrier, (NZ - 1) + (NCENT - 1) + (NX - 1))

    def spread_z(buf, p, send, recv):
        def go(step, carry):
            remote(
                buf.at[p, x, z],
                buf.at[p, x, z],
                send.at[p],
                recv.at[p],
                at_zx((z + far_first(step)) % NZ, x),
            ).start()
            return carry

        lax.fori_loop(0, NZ - 1, go, 0)

    def spread_x(buf, p, send, recv):
        take(buf.at[p, x, pl.ds(0, NZ - 1)], recv[0].at[p])
        for k in (2, 1, 3):
            remote(
                buf.at[p, x], buf.at[p, x], send.at[p], recv[1].at[p], at_zx(z, (x + k) % NX)
            ).start()

    def each_part(body):
        def go(p, carry):
            body(p)
            return carry

        lax.fori_loop(0, PARTS, go, 0)

    each_part(lambda p: spread_z(first, p, gz_send, gz_recv))

    def row_copy(owner, device, send):
        block = pl.ds(pl.multiple_of(owner * ROWS, ROWS), ROWS)
        return remote(
            rows.at[block, :], rows.at[block, :], rows_send_sem.at[send], rows_recv_sem.at[owner], device
        )

    sibling = at_cent(y * NC + 1 - core)
    for send, k in enumerate((1, 3, 2)):
        row_copy(cent, at_cent(((y + k) % NY) * NC + core), send).start()
    row_copy(cent, sibling, 3).start()

    each_part(lambda p: spread_x(first, p, gx_send, (gz_recv, gx_recv)))

    for send, k in enumerate((1, 3, 2)):
        owner = ((y + k) % NY) * NC + core
        row_copy(owner, sibling, send).wait_recv()
        row_copy(owner, sibling, 4 + send).start()
    for k in range(NY):
        row_copy(((y + k) % NY) * NC + 1 - core, sibling, 0).wait_recv()

    def row_norms(j, carry):
        here = pl.ds(pl.multiple_of(j * LANES, LANES), LANES)
        part = jnp.zeros((LANES, LANES), F32)
        for i in range(D // LANES):
            block = rows[here, i * LANES : (i + 1) * LANES].astype(F32)
            part += block * block
        row_sq[:, here] = jnp.sum(part.T, axis=0, keepdims=True)
        return carry

    lax.fori_loop(0, TILES, row_norms, 0)

    def products(buf, recv):
        def part(p):
            take(buf.at[p, pl.ds(0, NX - 1)], recv.at[p])
            lo = pl.ds(pl.multiple_of(2 * W * p, 2 * W), W)
            hi = pl.ds(pl.multiple_of(2 * W * p + W, W), W)
            both = pl.ds(pl.multiple_of(2 * W * p, 2 * W), 2 * W)
            for i in range(NX):
                block = buf[p, i].astype(F32)
                left = block[:, :OWN].reshape(NZ * OWN, W)
                right = block[:, OWN:].reshape(NZ * OWN, W)
                here = slice(i * NZ * OWN, (i + 1) * NZ * OWN)
                operand[here, lo] = left.astype(BF16)
                operand[here, hi] = right.astype(BF16)
                square = left * left + right * right
                norm_part[here, :] = jnp.where(p == 0, square, norm_part[here, :] + square)

            def tile(t, carry):
                here = pl.ds(pl.multiple_of(t * 256, 256), 256)
                piece = lax.dot_general(
                    operand[:, both],
                    rows[here, both],
                    (((1,), (1,)), ((), ())),
                    preferred_element_type=F32,
                )
                acc[:, here] = jnp.where(p == 0, piece, acc[:, here] + piece)
                return carry

            lax.fori_loop(0, GROUP // 256, tile, 0)

        norm_part[...] = jnp.zeros_like(norm_part)
        acc[...] = jnp.zeros_like(acc)
        each_part(part)
        norm[...] = jnp.broadcast_to(
            jnp.sum(norm_part[...], axis=1, keepdims=True), (SLICE, LANES)
        )

    def score_tile(t):
        here = pl.ds(pl.multiple_of(t * LANES, LANES), LANES)
        return here, -(row_sq[:, here] - 2.0 * acc[:, here] + norm[...]) / SCALE

    products(first, gx_recv)

    def first_stats(t, carry):
        here, score = score_tile(t)
        top = jnp.max(score, axis=0, keepdims=True)
        weight = jnp.exp(score - top)
        acc[:, here] = weight
        stat_send[t // 4, pl.ds(t % 4, 1), :] = top
        stat_send[t // 4, pl.ds(4 + t % 4, 1), :] = jnp.sum(weight, axis=0, keepdims=True)
        return carry

    lax.fori_loop(0, TILES, first_stats, 0)
    for k in range(1, NCENT):
        remote(
            stat_send, stat_recv.at[cent], st_send.at[0], st_recv.at[0], at_cent((cent + k) % NCENT)
        ).start()
    stat_recv[cent] = stat_send[...]
    take(stat_recv.at[pl.ds(0, NCENT - 1)], st_recv.at[0])
    tops = [stat_recv[s, :, 0:4, :] for s in range(NCENT)]
    top = tops[0]
    for s in range(1, NCENT):
        top = jnp.maximum(top, tops[s])
    total = jnp.zeros_like(top)
    for s in range(NCENT):
        total += stat_recv[s, :, 4:8, :] * jnp.exp(tops[s] - top)
    factor[...] = jnp.exp(stat_send[:, 0:4, :] - top) / total

    norm_part[...] = jnp.zeros_like(norm_part)

    def responsibilities(t, carry):
        here = pl.ds(pl.multiple_of(t * LANES, LANES), LANES)
        value = (acc[:, here] * factor[t // 4, pl.ds(t % 4, 1), :]).astype(BF16)
        resp[:, here] = value
        norm_part[...] += value.astype(F32)
        return carry

    lax.fori_loop(0, TILES, responsibilities, 0)

    lane = lax.broadcasted_iota(jnp.int32, (NZ, OWN, LANES), 2)
    layer = lax.broadcasted_iota(jnp.int32, (NZ, OWN, LANES), 0)
    for i in range(NX):
        mass = jnp.sum(norm_part[i * NZ * OWN : (i + 1) * NZ * OWN, :], axis=1, keepdims=True)
        mass = jnp.broadcast_to(mass, (NZ * OWN, LANES)).reshape(NZ, OWN, LANES)
        count_send[i] = jnp.sum(jnp.where(lane == layer, mass, 0.0), axis=0)
    for k in (2, 1, 3):
        to = (x + k) % NX
        remote(
            count_send.at[to], count_recv.at[x], nx_send.at[0], nx_recv.at[0], at_zx(z, to)
        ).start()
    count_recv[x] = count_send[x]

    def sums_x(p):
        both = pl.ds(pl.multiple_of(2 * W * p, 2 * W), 2 * W)
        for i in range(NX):
            value = jnp.dot(
                resp[i * NZ * OWN : (i + 1) * NZ * OWN, :], rows[:, both], preferred_element_type=F32
            )
            left = value[:, :W].reshape(NZ, OWN, W)
            right = value[:, W:].reshape(NZ, OWN, W)
            packed = jnp.concatenate([left, right], axis=1)
            sums_f[p, i] = packed
            sums_send[p, i] = packed.astype(BF16)
        for k in (2, 1, 3):
            to = (x + k) % NX
            remote(
                sums_send.at[p, to], sums_recv.at[p, x], cx_send.at[p], cx_recv.at[p], at_zx(z, to)
            ).start()

    each_part(sums_x)

    take(count_recv.at[pl.ds(0, NX - 1)], nx_recv.at[0])
    total_send[...] = (count_recv[0] + count_recv[1]) + (count_recv[2] + count_recv[3])

    def send_total(step, carry):
        remote(
            total_send,
            total_recv.at[z],
            nz_send.at[0],
            nz_recv.at[0],
            at_zx((z + far_first(step)) % NZ, x),
        ).start()
        return carry

    lax.fori_loop(0, NZ - 1, send_total, 0)
    total_recv[z] = total_send[...]

    def sums_z(p):
        take(sums_recv.at[p, pl.ds(0, NX - 1)], cx_recv.at[p])
        value = sums_f[p, x]
        for k in range(1, NX):
            value += sums_recv[p, (x + k) % NX].astype(F32)
        part_send[p] = value.astype(BF16)

        def go(step, carry):
            to = (z + far_first(step)) % NZ
            remote(
                part_send.at[p, to], part_recv.at[p, z], cz_send.at[p], cz_recv.at[p], at_zx(to, x)
            ).start()
            return carry

        lax.fori_loop(0, NZ - 1, go, 0)
        part_recv[p, z] = part_send[p, z]

    each_part(sums_z)

    take(total_recv.at[pl.ds(0, NZ - 1)], nz_recv.at[0])
    mass = jnp.sum(total_recv[...], axis=0)
    own_lane = lax.broadcasted_iota(jnp.int32, (OWN, LANES), 1) == z
    mass = jnp.sum(jnp.where(own_lane, mass, 0.0), axis=1, keepdims=True) + prior_mass

    def renew(p):
        take(part_recv.at[p, pl.ds(0, NZ - 1)], cz_recv.at[p])
        value = jnp.sum(part_recv[p].astype(F32), axis=0)
        lo = pl.ds(pl.multiple_of(2 * W * p, 2 * W), W)
        hi = pl.ds(pl.multiple_of(2 * W * p + W, W), W)
        left = (value[:OWN] + prior_mass * cent_v[:, lo]) / mass
        right = (value[OWN:] + prior_mass * cent_v[:, hi]) / mass
        upd_out[:, lo] = left
        upd_out[:, hi] = right
        second[p, x, z] = jnp.concatenate([left, right], axis=0).astype(BF16)
        spread_z(second, p, uz_send, uz_recv)

    each_part(renew)
    each_part(lambda p: spread_x(second, p, ux_send, (uz_recv, ux_recv)))
    products(second, ux_recv)

    def second_stats(t, carry):
        here, score = score_tile(t)
        top = jnp.max(score, axis=0, keepdims=True)
        shifted = score - top
        weight = jnp.exp(shifted)
        stat2_send[t, 0:1, :] = top
        stat2_send[t, 1:2, :] = jnp.sum(weight, axis=0, keepdims=True)
        stat2_send[t, 2:3, :] = jnp.sum(weight * shifted, axis=0, keepdims=True)
        return carry

    lax.fori_loop(0, TILES, second_stats, 0)

    def chip_tiles(chip):
        return pl.ds(chip * CHIP_TILES, CHIP_TILES)

    for k in range(1, NCENT):
        to = (cent + k) % NCENT
        remote(
            stat2_send.at[chip_tiles(to // NC)],
            stat2_recv.at[cent],
            st2_send.at[0],
            st2_recv.at[0],
            at_cent(to),
        ).start()
    stat2_recv[cent] = stat2_send[chip_tiles(y)]
    take(stat2_recv.at[pl.ds(0, NCENT - 1)], st2_recv.at[0])
    tops = [stat2_recv[s, :, 0:1, :] for s in range(NCENT)]
    top = tops[0]
    for s in range(1, NCENT):
        top = jnp.maximum(top, tops[s])
    total = jnp.zeros_like(top)
    spread = jnp.zeros_like(top)
    for s in range(NCENT):
        gap = tops[s] - top
        scale = jnp.exp(gap)
        mine = stat2_recv[s, :, 1:2, :]
        total += scale * mine
        spread += scale * (stat2_recv[s, :, 2:3, :] + gap * mine)
    ent_out[...] = jnp.log(total) - spread / total

    for send in range(7):
        row_copy(cent, sibling, send).wait_send()
    take(stat_recv.at[pl.ds(0, NCENT - 1)], st_send.at[0])
    take(stat2_recv.at[pl.ds(0, NCENT - 1)], st2_send.at[0])
    take(count_recv.at[pl.ds(0, NX - 1)], nx_send.at[0])
    take(total_recv.at[pl.ds(0, NZ - 1)], nz_send.at[0])

    def drain(p):
        take(first.at[p, 0, pl.ds(0, NZ - 1)], gz_send.at[p])
        take(first.at[p, pl.ds(0, NX - 1)], gx_send.at[p])
        take(sums_recv.at[p, pl.ds(0, NX - 1)], cx_send.at[p])
        take(part_recv.at[p, pl.ds(0, NZ - 1)], cz_send.at[p])
        take(second.at[p, 0, pl.ds(0, NZ - 1)], uz_send.at[p])
        take(second.at[p, pl.ds(0, NX - 1)], ux_send.at[p])

    each_part(drain)


def on_device(embeddings, centroids):
    vmem = pltpu.VMEM
    dma = pltpu.SemaphoreType.DMA
    gathered = (PARTS, NX, NZ, 2 * OWN, W)
    updated, entropy = pl.pallas_call(
        kernel,
        out_shape=(
            jax.ShapeDtypeStruct((OWN, D), F32),
            jax.ShapeDtypeStruct((CHIP_TILES, 1, LANES), F32),
        ),
        in_specs=[pl.BlockSpec(memory_space=pl.ANY)] * 2,
        out_specs=(pl.BlockSpec(memory_space=vmem), pl.BlockSpec(memory_space=vmem)),
        scratch_shapes=[
            vmem((ROWS, D), F32),
            vmem((OWN, D), F32),
            vmem((GROUP, D), BF16),
            vmem(gathered, BF16),
            vmem(gathered, BF16),
            vmem((SLICE, D), BF16),
            vmem((SLICE, LANES), F32),
            vmem((SLICE, LANES), F32),
            vmem((1, GROUP), F32),
            vmem((SLICE, GROUP), F32),
            vmem((SLICE, GROUP), BF16),
            vmem((3, 8, LANES), F32),
            vmem((NCENT, 3, 8, LANES), F32),
            vmem((3, 4, LANES), F32),
            vmem((TILES, 8, LANES), F32),
            vmem((NCENT, CHIP_TILES, 8, LANES), F32),
            vmem(gathered, F32),
            vmem(gathered, BF16),
            vmem(gathered, BF16),
            vmem((PARTS, NZ, 2 * OWN, W), BF16),
            vmem((PARTS, NZ, 2 * OWN, W), BF16),
            vmem((NX, OWN, LANES), F32),
            vmem((NX, OWN, LANES), F32),
            vmem((OWN, LANES), F32),
            vmem((NZ, OWN, LANES), F32),
            dma((2,)),
            dma((7,)),
            dma((NCENT,)),
        ]
        + [dma((PARTS,))] * 4
        + [dma((1,))] * 2
        + [dma((PARTS,))] * 4
        + [dma((1,))] * 4
        + [dma((PARTS,))] * 4
        + [dma((1,))] * 2,
        compiler_params=pltpu.CompilerParams(
            collective_id=0, has_side_effects=True, vmem_limit_bytes=48 * 2**20
        ),
        name="em_update",
    )(embeddings, centroids)
    core = lax.axis_index("cent") % NC
    entropy = lax.dynamic_slice_in_dim(entropy.reshape(CHIP), core * ROWS, ROWS, 0)
    return updated, entropy


def solution(mesh):
    in_specs = (P(("dp", "cent"), None), P(("dp", "cent"), None))
    out_specs = (P(("dp", "cent"), None), P(("dp", "cent")))
    return jax.shard_map(
        on_device, mesh=mesh, in_specs=in_specs, out_specs=out_specs, check_vma=False
    )
```

time: 556 us -> 106 us (0.19)
  waiting for transfers between devices: 332 us -> 0 us
  blocking collectives: 185 us -> 0 us
  Pallas kernels: 0 us -> 102 us
  between operations: 13.8 us -> 0.66 us
  other arithmetic: 11.1 us -> 0.02 us
  matrix products: 9.08 us -> 0 us
    all_gather x2 -> x0, waiting for transfers between devices: 179 us -> none  [the longest x1 138 us: on_device(): previous = lax.all_gather(centroids, 'dp', axis=0, tiled=True)]
    psum x1 -> x0, waiting for transfers between devices: 151 us -> none  [on_device(): sums, counts = lax.psum((sums, counts), 'dp')]
    psum x3 -> x0, blocking collectives: 151 us -> none  [the longest x1 116 us: on_device(): sums, counts = lax.psum((sums, counts), 'dp')]
    pallas_call x0 -> x1, Pallas kernels: none -> 102 us  [on_device(): pl.pallas_call(kernel, out_shape=(jax.ShapeDtypeStruct((OWN, D), F32), ja...]
    pmax x2 -> x0, blocking collectives: 34.2 us -> none  [row_stats(): top = lax.pmax(jnp.max(score, axis=1), 'cent')]
    dot_general x3 -> x0, matrix products: 9.08 us -> none  [the longest x2 5.9 us: score_piece(): jnp.einsum('rd,kd->rk', rows_b, piece, preferred_element_type=jnp.float32)]
    dot_general x3 -> x0, other arithmetic: 6.72 us -> none  [the longest x2 4 us: score_piece(): jnp.einsum('kd,kd->k', piece, piece, preferred_element_type=jnp.float32)]
  transfers between devices with their start and end apart: 3 -> 0, of which waited for: 3 -> 0; matrix products, arithmetic and copies ran while one was open for 1% -> 0% of each run, Pallas kernels for 0% -> 0%
where the time goes in v1:
time: 106 us; the launch traced here: 105 us
  Pallas kernels  102 us (96%)
  local copies, waits for them, and re-layouts  3.12 us (3%)
    pallas_call x1, Pallas kernels, on_device(): pl.pallas_call(kernel, out_shape=(jax.ShapeDtypeStruct((OWN, D), F32), ja...  102 us
    unnamed x5, local copies, waits for them, and re-layouts  2.48 us

profile of v1, /device:TPU:1, one launch (start us, length us, event | category | flops | bytes accessed | tf_op | source)
XLA Modules:
  0.0 105.5 jit_solution(11073402727269435208)
XLA Ops:
  0.6 0.0 copy-start.1
  0.7 0.7 copy-done.1
  1.4 0.0 copy-start
  1.4 1.1 %copy-done = f32[192,1024]{1,0:T(8,128)S(1)} copy-done((f32[192,1024]{1,0:T(8,128)S(1)}, f32[192,1024]{1,0:T(8,128)}, u32[]{:S(2)}) %copy-start) | copy-done | bytes 786456
  2.5 101.7 %em_update.1 = (f32[8,1024]{1,0:T(8,128)S(1)}, f32[3,1,128]{2,1,0:T(1,128)S(1)}) custom-call(f32[192,1024]{1,0:T(8,128)S(1)} %copy-done, f32[8,1024]{1,0:T(8,128)S(1)} %copy-done.1), custom_call_target="tpu_custom_call" | custom-call | tf_op jit(solution)/shard_map/em_update/pallas_call | solution.py:436
  104.2 0.6 dynamic_slice.3
  104.9 0.6 copy.5
  (1 shorter events, 0.0 us)
Async XLA Ops:
  0.6 0.8 copy-start.1
  1.4 1.1 %copy-start = (f32[192,1024]{1,0:T(8,128)S(1)}, f32[192,1024]{1,0:T(8,128)}, u32[]{:S(2)}) copy-start(f32[192,1024]{1,0:T(8,128)} %emb_hbm.1) | copy-start | bytes 2359300

commit v2 on v1

v2 whole, which is shorter than its diff:
```python
import jax
import jax.numpy as jnp
from jax import lax
from jax.experimental import pallas as pl
from jax.experimental.pallas import tpu as pltpu
from jax.sharding import PartitionSpec as P

MESH = pl.DeviceIdType.MESH
F32 = jnp.float32
BF16 = jnp.bfloat16

softness_level = 32.0
prior_mass = 4.0

D = 1024
NZ, NX, NY, NC = 16, 4, 4, 2
NCENT = NY * NC
ROWS = 192
GROUP = ROWS * NCENT
CHIP = ROWS * NC
OWN = 8
SLICE = OWN * NZ * NX
PARTS = 4
W = D // (2 * PARTS)
LANES = 128
TILES = GROUP // LANES
CHIP_TILES = CHIP // LANES
SCALE = 2.0 * softness_level
OFFSETS = (8, 7, 9, 6, 10, 5, 11, 4, 12, 3, 13, 2, 14, 1, 15, 0)
SLOT = {offset: slot for slot, offset in enumerate(OFFSETS)}
BACK = tuple(SLOT[(NZ - offset) % NZ] for offset in OFFSETS)
GROUPS = 4
PER = NZ // GROUPS
HOME = NZ - 1
HALF = ROWS // 2


def place():
    dp = lax.axis_index("dp")
    cent = lax.axis_index("cent")
    z = dp // NX
    x = dp % NX
    y = cent // NC
    core = cent % NC
    return z, x, y, core, cent


def kernel(
    emb_hbm,
    cent_hbm,
    upd_out,
    ent_out,
    emb_v,
    cent_v,
    rows,
    first,
    second,
    operand,
    norm_part,
    norm,
    row_sq,
    acc,
    resp,
    stat_send,
    stat_recv,
    factor,
    stat2_send,
    stat2_recv,
    sums_f,
    sums_send,
    sums_recv,
    part_send,
    part_recv,
    count_send,
    count_recv,
    total_send,
    total_recv,
    load_sem,
    rows_send_sem,
    rows_recv_sem,
    gz_send,
    gz_recv,
    gx_send,
    gx_recv,
    st_send,
    st_recv,
    cx_send,
    cx_recv,
    cz_send,
    cz_recv,
    nx_send,
    nx_recv,
    nz_send,
    nz_recv,
    uz_send,
    uz_recv,
    ux_send,
    ux_recv,
    st2_send,
    st2_recv,
):
    z, x, y, core, cent = place()

    def at_zx(z_to, x_to):
        return {"dp": z_to * NX + x_to, "cent": cent}

    def at_cent(cent_to):
        return {"dp": z * NX + x, "cent": cent_to}

    def remote(src, dst, send, recv, device):
        return pltpu.make_async_remote_copy(
            src_ref=src, dst_ref=dst, send_sem=send, recv_sem=recv, device_id=device, device_id_type=MESH
        )

    def take(ref, sem):
        pltpu.make_async_copy(ref, ref, sem).wait()

    pending = []

    def finish():
        for wait in pending:
            wait()

    def z_peer(slot):
        return lax.rem(z + OFFSETS[slot], NZ)

    barrier = pltpu.get_barrier_semaphore()
    for slot in range(HOME):
        pl.semaphore_signal(
            barrier, inc=1, device_id=at_zx(z_peer(slot), x), device_id_type=MESH
        )
    for k in range(1, NCENT):
        pl.semaphore_signal(
            barrier, inc=1, device_id=at_cent((cent + k) % NCENT), device_id_type=MESH
        )
    for k in range(1, NX):
        pl.semaphore_signal(barrier, inc=1, device_id=at_zx(z, (x + k) % NX), device_id_type=MESH)

    load_cent = pltpu.make_async_copy(cent_hbm, cent_v, load_sem.at[0])
    load_emb = pltpu.make_async_copy(emb_hbm, emb_v, load_sem.at[1])
    load_cent.start()
    load_emb.start()

    load_cent.wait()
    for p in range(PARTS):
        left = cent_v[:, 2 * W * p : 2 * W * p + W]
        right = cent_v[:, 2 * W * p + W : 2 * W * (p + 1)]
        first[p, x, HOME] = jnp.concatenate([left, right], axis=0).astype(BF16)
    load_emb.wait()
    own_rows = pl.ds(pl.multiple_of(cent * ROWS, ROWS), ROWS)
    rows[own_rows, :] = emb_v[...].astype(BF16)

    pl.semaphore_wait(barrier, (NZ - 1) + (NCENT - 1) + (NX - 1))

    def row_copy(owner, half, device, send):
        block = pl.ds(pl.multiple_of(owner * ROWS + half * HALF, HALF), HALF)
        return remote(
            rows.at[block, :],
            rows.at[block, :],
            rows_send_sem.at[send],
            rows_recv_sem.at[owner, half],
            device,
        )

    def owner_at(k):
        return lax.rem(y + k, NY) * NC + core

    up, down, far = owner_at(1), owner_at(3), owner_at(2)
    to_up, to_down, sibling = at_cent(up), at_cent(down), at_cent(y * NC + 1 - core)
    row_copy(cent, 0, to_up, 0).start()
    row_copy(cent, 1, to_down, 1).start()
    row_copy(cent, 1, to_up, 2).start()
    row_copy(cent, 0, to_down, 3).start()
    row_copy(cent, 0, sibling, 4).start()
    row_copy(cent, 1, sibling, 5).start()
    pending.append(lambda: [row_copy(cent, 0, sibling, k).wait_send() for k in range(14)])

    def spread_z(buf, p, send, recv):
        for slot in range(HOME):
            there = BACK[slot]
            remote(
                buf.at[p, x, HOME],
                buf.at[p, x, there],
                send.at[p],
                recv.at[p, there // PER],
                at_zx(z_peer(slot), x),
            ).start()

    def spread_x(buf, p, send, recv):
        for g in reversed(range(GROUPS)):
            count = PER - (g == GROUPS - 1)
            group = pl.ds(g * PER, PER)
            take(buf.at[p, x, pl.ds(g * PER, count)], recv[0].at[p, g])
            for k in (2, 1, 3):
                remote(
                    buf.at[p, x, group],
                    buf.at[p, x, group],
                    send.at[p],
                    recv[1].at[p],
                    at_zx(z, lax.rem(x + k, NX)),
                ).start()

    def each_part(body, start=0, stop=PARTS):
        def go(p, carry):
            body(p)
            return carry

        lax.fori_loop(start, stop, go, 0)

    each_part(lambda p: spread_z(first, p, gz_send, gz_recv))
    pending.append(lambda: each_part(lambda p: take(first.at[p, 0, pl.ds(0, NZ - 1)], gz_send.at[p])))

    spread_first = lambda p: spread_x(first, p, gx_send, (gz_recv, gx_recv))
    each_part(spread_first, 0, 1)
    row_copy(down, 0, sibling, 0).wait_recv()
    row_copy(down, 0, to_up, 6).start()
    row_copy(up, 1, sibling, 0).wait_recv()
    row_copy(up, 1, to_down, 7).start()
    row_copy(down, 0, sibling, 8).start()
    row_copy(up, 1, sibling, 9).start()
    each_part(spread_first, 1, 3)
    row_copy(down, 1, sibling, 0).wait_recv()
    row_copy(down, 1, sibling, 10).start()
    row_copy(up, 0, sibling, 0).wait_recv()
    row_copy(up, 0, sibling, 11).start()
    each_part(spread_first, 3, 4)
    pending.append(lambda: each_part(lambda p: take(first.at[p, pl.ds(0, NX - 1)], gx_send.at[p])))
    for half in range(2):
        row_copy(far, half, sibling, 0).wait_recv()
        row_copy(far, half, sibling, 12 + half).start()
    for k in range(NY):
        for half in range(2):
            row_copy(lax.rem(y + k, NY) * NC + 1 - core, half, sibling, 0).wait_recv()

    def row_norms(j, carry):
        here = pl.ds(pl.multiple_of(j * LANES, LANES), LANES)
        part = jnp.zeros((LANES, LANES), F32)
        for i in range(D // LANES):
            block = rows[here, i * LANES : (i + 1) * LANES].astype(F32)
            part += block * block
        row_sq[:, here] = jnp.sum(part.T, axis=0, keepdims=True)
        return carry

    lax.fori_loop(0, TILES, row_norms, 0)

    def products(buf, recv):
        def part(p):
            take(buf.at[p, pl.ds(0, NX - 1)], recv.at[p])
            lo = pl.ds(pl.multiple_of(2 * W * p, 2 * W), W)
            hi = pl.ds(pl.multiple_of(2 * W * p + W, W), W)
            both = pl.ds(pl.multiple_of(2 * W * p, 2 * W), 2 * W)
            for i in range(NX):
                block = buf[p, i].astype(F32)
                left = block[:, :OWN].reshape(NZ * OWN, W)
                right = block[:, OWN:].reshape(NZ * OWN, W)
                here = slice(i * NZ * OWN, (i + 1) * NZ * OWN)
                operand[here, lo] = left.astype(BF16)
                operand[here, hi] = right.astype(BF16)
                norm_part[here, :] += left * left + right * right
            acc[...] += lax.dot_general(
                operand[:, both],
                rows[:, both],
                (((1,), (1,)), ((), ())),
                preferred_element_type=F32,
            )

        each_part(part)
        norm[...] = jnp.broadcast_to(
            jnp.sum(norm_part[...], axis=1, keepdims=True), (SLICE, LANES)
        )

    def score_tile(t):
        here = slice(t * LANES, (t + 1) * LANES)
        return here, -(row_sq[:, here] - 2.0 * acc[:, here] + norm[...]) / SCALE

    norm_part[...] = jnp.zeros_like(norm_part)
    acc[...] = jnp.zeros_like(acc)
    products(first, gx_recv)

    for t in range(TILES):
        here, score = score_tile(t)
        top = jnp.max(score, axis=0, keepdims=True)
        weight = jnp.exp(score - top)
        acc[:, here] = weight
        stat_send[t // 4, t % 4 : t % 4 + 1, :] = top
        stat_send[t // 4, 4 + t % 4 : 5 + t % 4, :] = jnp.sum(weight, axis=0, keepdims=True)
    for k in range(1, NCENT):
        remote(
            stat_send, stat_recv.at[cent], st_send.at[0], st_recv.at[0], at_cent((cent + k) % NCENT)
        ).start()
    pending.append(lambda: take(stat_recv.at[pl.ds(0, NCENT - 1)], st_send.at[0]))
    stat_recv[cent] = stat_send[...]
    take(stat_recv.at[pl.ds(0, NCENT - 1)], st_recv.at[0])
    tops = [stat_recv[s, :, 0:4, :] for s in range(NCENT)]
    top = tops[0]
    for s in range(1, NCENT):
        top = jnp.maximum(top, tops[s])
    total = jnp.zeros_like(top)
    for s in range(NCENT):
        total += stat_recv[s, :, 4:8, :] * jnp.exp(tops[s] - top)
    factor[...] = jnp.exp(stat_send[:, 0:4, :] - top) / total

    for t in range(TILES):
        here = slice(t * LANES, (t + 1) * LANES)
        resp[:, here] = (acc[:, here] * factor[t // 4, t % 4 : t % 4 + 1, :]).astype(BF16)

    def sums_x(p):
        both = pl.ds(pl.multiple_of(2 * W * p, 2 * W), 2 * W)
        value = jnp.dot(resp[...], rows[:, both], preferred_element_type=F32)
        for i in range(NX):
            block = value[i * NZ * OWN : (i + 1) * NZ * OWN]
            left = block[:, :W].reshape(NZ, OWN, W)
            right = block[:, W:].reshape(NZ, OWN, W)
            packed = jnp.concatenate([left, right], axis=1)
            sums_f[p, i] = packed
            sums_send[p, i] = packed.astype(BF16)
        for g in range(GROUPS):
            group = pl.ds(g * PER, PER)
            for k in (2, 1, 3):
                to = lax.rem(x + k, NX)
                remote(
                    sums_send.at[p, to, group],
                    sums_recv.at[p, x, group],
                    cx_send.at[p],
                    cx_recv.at[p, g],
                    at_zx(z, to),
                ).start()

    each_part(sums_x, 0, 1)

    mass_part = jnp.zeros((SLICE, LANES), F32)
    for t in range(TILES):
        mass_part += resp[:, t * LANES : (t + 1) * LANES].astype(F32)
    norm_part[...] = mass_part
    lane = lax.broadcasted_iota(jnp.int32, (NZ, OWN, LANES), 2)
    layer = lax.broadcasted_iota(jnp.int32, (NZ, OWN, LANES), 0)
    for i in range(NX):
        mass = jnp.sum(norm_part[i * NZ * OWN : (i + 1) * NZ * OWN, :], axis=1, keepdims=True)
        mass = jnp.broadcast_to(mass, (NZ * OWN, LANES)).reshape(NZ, OWN, LANES)
        count_send[i] = jnp.sum(jnp.where(lane == layer, mass, 0.0), axis=0)
    for k in (2, 1, 3):
        to = lax.rem(x + k, NX)
        remote(
            count_send.at[to], count_recv.at[x], nx_send.at[0], nx_recv.at[0], at_zx(z, to)
        ).start()
    pending.append(lambda: take(count_recv.at[pl.ds(0, NX - 1)], nx_send.at[0]))
    count_recv[x] = count_send[x]

    each_part(sums_x, 1, PARTS)
    pending.append(lambda: each_part(lambda p: take(sums_recv.at[p, pl.ds(0, NX - 1)], cx_send.at[p])))

    def sums_z(p):
        for g in range(GROUPS):
            group = slice(g * PER, (g + 1) * PER)
            take(sums_recv.at[p, pl.ds(0, NX - 1), pl.ds(g * PER, PER)], cx_recv.at[p, g])
            value = sums_f[p, x, group]
            for k in range(1, NX):
                value += sums_recv[p, lax.rem(x + k, NX), group].astype(F32)
            part_send[p, group] = value.astype(BF16)
            for slot in range(g * PER, (g + 1) * PER):
                if slot != HOME:
                    remote(
                        part_send.at[p, slot],
                        part_recv.at[p, BACK[slot]],
                        cz_send.at[p],
                        cz_recv.at[p],
                        at_zx(z_peer(slot), x),
                    ).start()
        part_recv[p, HOME] = part_send[p, HOME]

    each_part(sums_z, 0, 2)

    take(count_recv.at[pl.ds(0, NX - 1)], nx_recv.at[0])
    total_send[...] = (count_recv[0] + count_recv[1]) + (count_recv[2] + count_recv[3])
    for slot in range(HOME):
        remote(
            total_send,
            total_recv.at[BACK[slot]],
            nz_send.at[0],
            nz_recv.at[0],
            at_zx(z_peer(slot), x),
        ).start()
    pending.append(lambda: take(total_recv.at[pl.ds(0, NZ - 1)], nz_send.at[0]))
    total_recv[HOME] = total_send[...]

    each_part(sums_z, 2, PARTS)
    pending.append(lambda: each_part(lambda p: take(part_recv.at[p, pl.ds(0, NZ - 1)], cz_send.at[p])))

    norm_part[...] = jnp.zeros_like(norm_part)
    acc[...] = jnp.zeros_like(acc)

    take(total_recv.at[pl.ds(0, NZ - 1)], nz_recv.at[0])
    lane = lax.broadcasted_iota(jnp.int32, (OWN, LANES), 1)
    mass = jnp.zeros((OWN, LANES), F32)
    for slot in range(NZ):
        mass += jnp.where(lane == BACK[slot], total_recv[slot], 0.0)
    mass = jnp.sum(mass, axis=1, keepdims=True) + prior_mass

    def renew(p):
        take(part_recv.at[p, pl.ds(0, NZ - 1)], cz_recv.at[p])
        value = jnp.sum(part_recv[p].astype(F32), axis=0)
        lo = pl.ds(pl.multiple_of(2 * W * p, 2 * W), W)
        hi = pl.ds(pl.multiple_of(2 * W * p + W, W), W)
        left = (value[:OWN] + prior_mass * cent_v[:, lo]) / mass
        right = (value[OWN:] + prior_mass * cent_v[:, hi]) / mass
        upd_out[:, lo] = left
        upd_out[:, hi] = right
        second[p, x, HOME] = jnp.concatenate([left, right], axis=0).astype(BF16)
        spread_z(second, p, uz_send, uz_recv)

    each_part(renew)
    pending.append(lambda: each_part(lambda p: take(second.at[p, 0, pl.ds(0, NZ - 1)], uz_send.at[p])))
    each_part(lambda p: spread_x(second, p, ux_send, (uz_recv, ux_recv)))
    pending.append(lambda: each_part(lambda p: take(second.at[p, pl.ds(0, NX - 1)], ux_send.at[p])))
    products(second, ux_recv)

    for t in range(TILES):
        here, score = score_tile(t)
        top = jnp.max(score, axis=0, keepdims=True)
        shifted = score - top
        weight = jnp.exp(shifted)
        stat2_send[t, 0:1, :] = top
        stat2_send[t, 1:2, :] = jnp.sum(weight, axis=0, keepdims=True)
        stat2_send[t, 2:3, :] = jnp.sum(weight * shifted, axis=0, keepdims=True)

    def chip_tiles(chip):
        return pl.ds(chip * CHIP_TILES, CHIP_TILES)

    for k in range(1, NCENT):
        to = (cent + k) % NCENT
        remote(
            stat2_send.at[chip_tiles(to // NC)],
            stat2_recv.at[cent],
            st2_send.at[0],
            st2_recv.at[0],
            at_cent(to),
        ).start()
    pending.append(lambda: take(stat2_recv.at[pl.ds(0, NCENT - 1)], st2_send.at[0]))
    stat2_recv[cent] = stat2_send[chip_tiles(y)]
    take(stat2_recv.at[pl.ds(0, NCENT - 1)], st2_recv.at[0])
    tops = [stat2_recv[s, :, 0:1, :] for s in range(NCENT)]
    top = tops[0]
    for s in range(1, NCENT):
        top = jnp.maximum(top, tops[s])
    total = jnp.zeros_like(top)
    spread = jnp.zeros_like(top)
    for s in range(NCENT):
        gap = tops[s] - top
        scale = jnp.exp(gap)
        mine = stat2_recv[s, :, 1:2, :]
        total += scale * mine
        spread += scale * (stat2_recv[s, :, 2:3, :] + gap * mine)
    ent_out[...] = jnp.log(total) - spread / total

    finish()


def on_device(embeddings, centroids):
    vmem = pltpu.VMEM
    dma = pltpu.SemaphoreType.DMA
    gathered = (PARTS, NX, NZ, 2 * OWN, W)
    updated, entropy = pl.pallas_call(
        kernel,
        out_shape=(
            jax.ShapeDtypeStruct((OWN, D), F32),
            jax.ShapeDtypeStruct((CHIP_TILES, 1, LANES), F32),
        ),
        in_specs=[pl.BlockSpec(memory_space=pl.ANY)] * 2,
        out_specs=(pl.BlockSpec(memory_space=vmem), pl.BlockSpec(memory_space=vmem)),
        scratch_shapes=[
            vmem((ROWS, D), F32),
            vmem((OWN, D), F32),
            vmem((GROUP, D), BF16),
            vmem(gathered, BF16),
            vmem(gathered, BF16),
            vmem((SLICE, D), BF16),
            vmem((SLICE, LANES), F32),
            vmem((SLICE, LANES), F32),
            vmem((1, GROUP), F32),
            vmem((SLICE, GROUP), F32),
            vmem((SLICE, GROUP), BF16),
            vmem((3, 8, LANES), F32),
            vmem((NCENT, 3, 8, LANES), F32),
            vmem((3, 4, LANES), F32),
            vmem((TILES, 8, LANES), F32),
            vmem((NCENT, CHIP_TILES, 8, LANES), F32),
            vmem(gathered, F32),
            vmem(gathered, BF16),
            vmem(gathered, BF16),
            vmem((PARTS, NZ, 2 * OWN, W), BF16),
            vmem((PARTS, NZ, 2 * OWN, W), BF16),
            vmem((NX, OWN, LANES), F32),
            vmem((NX, OWN, LANES), F32),
            vmem((OWN, LANES), F32),
            vmem((NZ, OWN, LANES), F32),
            dma((2,)),
            dma((14,)),
            dma((NCENT, 2)),
            dma((PARTS,)),
            dma((PARTS, GROUPS)),
            dma((PARTS,)),
            dma((PARTS,)),
            dma((1,)),
            dma((1,)),
            dma((PARTS,)),
            dma((PARTS, GROUPS)),
            dma((PARTS,)),
            dma((PARTS,)),
            dma((1,)),
            dma((1,)),
            dma((1,)),
            dma((1,)),
            dma((PARTS,)),
            dma((PARTS, GROUPS)),
            dma((PARTS,)),
            dma((PARTS,)),
            dma((1,)),
            dma((1,)),
        ],
        compiler_params=pltpu.CompilerParams(
            collective_id=0, has_side_effects=True, vmem_limit_bytes=63 * 2**20
        ),
        name="em_update",
    )(embeddings, centroids)
    core = lax.axis_index("cent") % NC
    entropy = lax.dynamic_slice_in_dim(entropy.reshape(CHIP), core * ROWS, ROWS, 0)
    return updated, entropy


def solution(mesh):
    in_specs = (P(("dp", "cent"), None), P(("dp", "cent"), None))
    out_specs = (P(("dp", "cent"), None), P(("dp", "cent")))
    return jax.shard_map(
        on_device, mesh=mesh, in_specs=in_specs, out_specs=out_specs, check_vma=False
    )
```

time: 106 us -> 93.2 us (0.88)
  Pallas kernels: 102 us -> 89.6 us
    pallas_call x1, Pallas kernels: 102 us -> 89.6 us  [on_device(): pl.pallas_call(kernel, out_shape=(jax.ShapeDtypeStruct((OWN, D), F32), ja...]
    unnamed x5 -> x3, local copies, waits for them, and re-layouts: 2.48 us -> 2.02 us
where the time goes in v2:
time: 93.2 us; the launch traced here: 93 us
  Pallas kernels  89.6 us (96%)
  local copies, waits for them, and re-layouts  2.66 us (3%)
    pallas_call x1, Pallas kernels, on_device(): pl.pallas_call(kernel, out_shape=(jax.ShapeDtypeStruct((OWN, D), F32), ja...  89.6 us
    unnamed x3, local copies, waits for them, and re-layouts  2.02 us

profile of v2, /device:TPU:1, one launch (start us, length us, event | category | flops | bytes accessed | tf_op | source)
XLA Modules:
  0.0 93.0 jit_solution(13061034604714450606)
XLA Ops:
  0.6 89.6 %em_update.1 = (f32[8,1024]{1,0:T(8,128)}, f32[3,1,128]{2,1,0:T(1,128)}) custom-call(f32[192,1024]{1,0:T(8,128)} %emb_hbm.1, f32[8,1024]{1,0:T(8,128)} %cent_hbm.1), custom_call_target="tpu_custom_call" | custom-call | tf_op jit(solution)/shard_map/em_update/pallas_call | solution.py:462
  90.3 0.0 copy-start
  90.3 0.6 copy-done
  90.9 0.6 dynamic_slice.3
  91.6 1.4 %copy.5 = f32[8,1024]{1,0:T(8,128)} copy(f32[8,1024]{1,0:T(8,128)} %get-tuple-element.8) | data formatting | bytes 65536
  (1 shorter events, 0.0 us)
Async XLA Ops:
  90.3 0.7 copy-start

commit v3 on v2

--- a/solution.py
+++ b/solution.py
@@ -169,11 +169,9 @@
     to_up, to_down, sibling = at_cent(up), at_cent(down), at_cent(y * NC + 1 - core)
     row_copy(cent, 0, to_up, 0).start()
     row_copy(cent, 1, to_down, 1).start()
-    row_copy(cent, 1, to_up, 2).start()
-    row_copy(cent, 0, to_down, 3).start()
     row_copy(cent, 0, sibling, 4).start()
     row_copy(cent, 1, sibling, 5).start()
-    pending.append(lambda: [row_copy(cent, 0, sibling, k).wait_send() for k in range(14)])
+    pending.append(lambda: [row_copy(cent, 0, sibling, k).wait_send() for k in range(2, 14)])
 
     def spread_z(buf, p, send, recv):
         for slot in range(HOME):
@@ -186,19 +184,21 @@
                 at_zx(z_peer(slot), x),
             ).start()
 
-    def spread_x(buf, p, send, recv):
-        for g in reversed(range(GROUPS)):
-            count = PER - (g == GROUPS - 1)
-            group = pl.ds(g * PER, PER)
-            take(buf.at[p, x, pl.ds(g * PER, count)], recv[0].at[p, g])
-            for k in (2, 1, 3):
-                remote(
-                    buf.at[p, x, group],
-                    buf.at[p, x, group],
-                    send.at[p],
-                    recv[1].at[p],
-                    at_zx(z, lax.rem(x + k, NX)),
-                ).start()
+    def spread_x(buf, p, g, send, recv):
+        group = pl.ds(g * PER, PER)
+        take(buf.at[p, x, pl.ds(g * PER, PER - (g == GROUPS - 1))], recv[0].at[p, g])
+        for k in (2, 1, 3):
+            remote(
+                buf.at[p, x, group],
+                buf.at[p, x, group],
+                send.at[p],
+                recv[1].at[p],
+                at_zx(z, lax.rem(x + k, NX)),
+            ).start()
+
+    def in_order(lag):
+        pieces = [(p, g) for p in range(PARTS) for g in range(GROUPS)]
+        return sorted(pieces, key=lambda piece: piece[0] + lag * (GROUPS - 1 - piece[1]))
 
     def each_part(body, start=0, stop=PARTS):
         def go(p, carry):
@@ -210,38 +210,53 @@
     each_part(lambda p: spread_z(first, p, gz_send, gz_recv))
     pending.append(lambda: each_part(lambda p: take(first.at[p, 0, pl.ds(0, NZ - 1)], gz_send.at[p])))
 
-    spread_first = lambda p: spread_x(first, p, gx_send, (gz_recv, gx_recv))
-    each_part(spread_first, 0, 1)
+    row_copy(cent, 0, to_up, 0).wait_send()
+    row_copy(cent, 1, to_up, 2).start()
+    row_copy(cent, 1, to_down, 1).wait_send()
+    row_copy(cent, 0, to_down, 3).start()
+
+    steps = in_order(0.6)
+
+    def spread_first(start, stop):
+        for p, g in steps[start:stop]:
+            spread_x(first, p, g, gx_send, (gz_recv, gx_recv))
+
+    def chip_norms(k):
+        chip = lax.rem(y + k, NY)
+        for half in range(2):
+            row_copy(chip * NC + 1 - core, half, sibling, 0).wait_recv()
+        for j in range(CHIP_TILES):
+            here = pl.ds(pl.multiple_of(chip * CHIP + j * LANES, LANES), LANES)
+            part = jnp.zeros((LANES, LANES), F32)
+            for i in range(D // LANES):
+                block = rows[here, i * LANES : (i + 1) * LANES].astype(F32)
+                part += block * block
+            row_sq[:, here] = jnp.sum(part.T, axis=0, keepdims=True)
+
+    spread_first(0, 2)
     row_copy(down, 0, sibling, 0).wait_recv()
     row_copy(down, 0, to_up, 6).start()
     row_copy(up, 1, sibling, 0).wait_recv()
     row_copy(up, 1, to_down, 7).start()
     row_copy(down, 0, sibling, 8).start()
     row_copy(up, 1, sibling, 9).start()
-    each_part(spread_first, 1, 3)
+    spread_first(2, 8)
     row_copy(down, 1, sibling, 0).wait_recv()
     row_copy(down, 1, sibling, 10).start()
     row_copy(up, 0, sibling, 0).wait_recv()
     row_copy(up, 0, sibling, 11).start()
-    each_part(spread_first, 3, 4)
+    spread_first(8, 12)
+    norm_part[...] = jnp.zeros_like(norm_part)
+    acc[...] = jnp.zeros_like(acc)
+    chip_norms(0)
+    spread_first(12, 16)
     pending.append(lambda: each_part(lambda p: take(first.at[p, pl.ds(0, NX - 1)], gx_send.at[p])))
+    chip_norms(1)
+    chip_norms(3)
     for half in range(2):
         row_copy(far, half, sibling, 0).wait_recv()
         row_copy(far, half, sibling, 12 + half).start()
-    for k in range(NY):
-        for half in range(2):
-            row_copy(lax.rem(y + k, NY) * NC + 1 - core, half, sibling, 0).wait_recv()
-
-    def row_norms(j, carry):
-        here = pl.ds(pl.multiple_of(j * LANES, LANES), LANES)
-        part = jnp.zeros((LANES, LANES), F32)
-        for i in range(D // LANES):
-            block = rows[here, i * LANES : (i + 1) * LANES].astype(F32)
-            part += block * block
-        row_sq[:, here] = jnp.sum(part.T, axis=0, keepdims=True)
-        return carry
-
-    lax.fori_loop(0, TILES, row_norms, 0)
+    chip_norms(2)
 
     def products(buf, recv):
         def part(p):
@@ -273,8 +288,6 @@
         here = slice(t * LANES, (t + 1) * LANES)
         return here, -(row_sq[:, here] - 2.0 * acc[:, here] + norm[...]) / SCALE
 
-    norm_part[...] = jnp.zeros_like(norm_part)
-    acc[...] = jnp.zeros_like(acc)
     products(first, gx_recv)
 
     for t in range(TILES):
@@ -408,9 +421,15 @@
         second[p, x, HOME] = jnp.concatenate([left, right], axis=0).astype(BF16)
         spread_z(second, p, uz_send, uz_recv)
 
-    each_part(renew)
+    renew(0)
+    renew(1)
+    done = 1
+    for p, g in in_order(0.9):
+        if done < min(p + 1 + (GROUPS - 1 - g) // 2, PARTS - 1) or done < p:
+            done += 1
+            renew(done)
+        spread_x(second, p, g, ux_send, (uz_recv, ux_recv))
     pending.append(lambda: each_part(lambda p: take(second.at[p, 0, pl.ds(0, NZ - 1)], uz_send.at[p])))
-    each_part(lambda p: spread_x(second, p, ux_send, (uz_recv, ux_recv)))
     pending.append(lambda: each_part(lambda p: take(second.at[p, pl.ds(0, NX - 1)], ux_send.at[p])))
     products(second, ux_recv)
 
@@ -437,6 +456,7 @@
         ).start()
     pending.append(lambda: take(stat2_recv.at[pl.ds(0, NCENT - 1)], st2_send.at[0]))
     stat2_recv[cent] = stat2_send[chip_tiles(y)]
+    finish()
     take(stat2_recv.at[pl.ds(0, NCENT - 1)], st2_recv.at[0])
     tops = [stat2_recv[s, :, 0:1, :] for s in range(NCENT)]
     top = tops[0]
@@ -451,8 +471,6 @@
         total += scale * mine
         spread += scale * (stat2_recv[s, :, 2:3, :] + gap * mine)
     ent_out[...] = jnp.log(total) - spread / total
-
-    finish()
 
 
 def on_device(embeddings, centroids):

time: 93.2 us -> 95.8 us (1.028)
  Pallas kernels: 89.6 us -> 92.2 us
    pallas_call x1, Pallas kernels: 89.6 us -> 92.2 us  [on_device(): pl.pallas_call(kernel, out_shape=(jax.ShapeDtypeStruct((OWN, D), F32), ja...]
where the time goes in v3:
time: 95.8 us; the launch traced here: 95.5 us
  Pallas kernels  92.2 us (96%)
  local copies, waits for them, and re-layouts  2.66 us (3%)
    pallas_call x1, Pallas kernels, on_device(): pl.pallas_call(kernel, out_shape=(jax.ShapeDtypeStruct((OWN, D), F32), ja...  92.2 us
    unnamed x3, local copies, waits for them, and re-layouts  2.02 us

profile of v3, /device:TPU:1, one launch (start us, length us, event | category | flops | bytes accessed | tf_op | source)
XLA Modules:
  0.0 95.5 jit_solution(1704670448906231880)
XLA Ops:
  0.6 92.2 %em_update.1 = (f32[8,1024]{1,0:T(8,128)}, f32[3,1,128]{2,1,0:T(1,128)}) custom-call(f32[192,1024]{1,0:T(8,128)} %emb_hbm.1, f32[8,1024]{1,0:T(8,128)} %cent_hbm.1), custom_call_target="tpu_custom_call" | custom-call | tf_op jit(solution)/shard_map/em_update/pallas_call | solution.py:480
  92.9 0.0 copy-start
  92.9 0.6 copy-done
  93.5 0.6 dynamic_slice.3
  94.2 1.4 %copy.5 = f32[8,1024]{1,0:T(8,128)} copy(f32[8,1024]{1,0:T(8,128)} %get-tuple-element.8) | data formatting | bytes 65536
  (1 shorter events, 0.0 us)
Async XLA Ops:
  92.9 0.7 copy-start

commit v4 on v3

--- a/solution.py
+++ b/solution.py
@@ -174,7 +174,7 @@
     pending.append(lambda: [row_copy(cent, 0, sibling, k).wait_send() for k in range(2, 14)])
 
     def spread_z(buf, p, send, recv):
-        for slot in range(HOME):
+        for slot in reversed(range(HOME)):
             there = BACK[slot]
             remote(
                 buf.at[p, x, HOME],
@@ -231,7 +231,7 @@
             for i in range(D // LANES):
                 block = rows[here, i * LANES : (i + 1) * LANES].astype(F32)
                 part += block * block
-            row_sq[:, here] = jnp.sum(part.T, axis=0, keepdims=True)
+            row_sq[:, here] = jnp.sum(part.T, axis=0, keepdims=True) * (1.0 / SCALE)
 
     spread_first(0, 2)
     row_copy(down, 0, sibling, 0).wait_recv()
@@ -281,41 +281,53 @@
 
         each_part(part)
         norm[...] = jnp.broadcast_to(
-            jnp.sum(norm_part[...], axis=1, keepdims=True), (SLICE, LANES)
+            jnp.sum(norm_part[...] * (1.0 / SCALE), axis=1, keepdims=True), (SLICE, LANES)
         )
 
-    def score_tile(t):
-        here = slice(t * LANES, (t + 1) * LANES)
-        return here, -(row_sq[:, here] - 2.0 * acc[:, here] + norm[...]) / SCALE
-
     products(first, gx_recv)
 
-    for t in range(TILES):
-        here, score = score_tile(t)
-        top = jnp.max(score, axis=0, keepdims=True)
-        weight = jnp.exp(score - top)
-        acc[:, here] = weight
-        stat_send[t // 4, t % 4 : t % 4 + 1, :] = top
-        stat_send[t // 4, 4 + t % 4 : 5 + t % 4, :] = jnp.sum(weight, axis=0, keepdims=True)
-    for k in range(1, NCENT):
-        remote(
-            stat_send, stat_recv.at[cent], st_send.at[0], st_recv.at[0], at_cent((cent + k) % NCENT)
-        ).start()
-    pending.append(lambda: take(stat_recv.at[pl.ds(0, NCENT - 1)], st_send.at[0]))
-    stat_recv[cent] = stat_send[...]
-    take(stat_recv.at[pl.ds(0, NCENT - 1)], st_recv.at[0])
-    tops = [stat_recv[s, :, 0:4, :] for s in range(NCENT)]
-    top = tops[0]
-    for s in range(1, NCENT):
-        top = jnp.maximum(top, tops[s])
-    total = jnp.zeros_like(top)
-    for s in range(NCENT):
-        total += stat_recv[s, :, 4:8, :] * jnp.exp(tops[s] - top)
-    factor[...] = jnp.exp(stat_send[:, 0:4, :] - top) / total
-
-    for t in range(TILES):
-        here = slice(t * LANES, (t + 1) * LANES)
-        resp[:, here] = (acc[:, here] * factor[t // 4, t % 4 : t % 4 + 1, :]).astype(BF16)
+    def score_at(here):
+        return (acc[:, here] * (2.0 / SCALE) - row_sq[:, here]) - norm[...]
+
+    def tile(t):
+        return slice(t * LANES, (t + 1) * LANES)
+
+    for h in range(2):
+        for j in range(TILES // 2):
+            here = tile(h * (TILES // 2) + j)
+            score = score_at(here)
+            top = jnp.max(score, axis=0, keepdims=True)
+            weight = jnp.exp(score - top)
+            acc[:, here] = weight
+            r = j % 3
+            stat_send[h, j // 3, r : r + 1, :] = top
+            stat_send[h, j // 3, 4 + r : 5 + r, :] = jnp.sum(weight, axis=0, keepdims=True)
+        for k in range(1, NCENT):
+            remote(
+                stat_send.at[h],
+                stat_recv.at[h, cent],
+                st_send.at[h],
+                st_recv.at[h],
+                at_cent(lax.rem(cent + k, NCENT)),
+            ).start()
+        stat_recv[h, cent] = stat_send[h]
+    pending.append(
+        lambda: [take(stat_recv.at[h, pl.ds(0, NCENT - 1)], st_send.at[h]) for h in range(2)]
+    )
+    for h in range(2):
+        take(stat_recv.at[h, pl.ds(0, NCENT - 1)], st_recv.at[h])
+        tops = [stat_recv[h, s, :, 0:3, :] for s in range(NCENT)]
+        top = tops[0]
+        for s in range(1, NCENT):
+            top = jnp.maximum(top, tops[s])
+        total = jnp.zeros_like(top)
+        for s in range(NCENT):
+            total += stat_recv[h, s, :, 4:7, :] * jnp.exp(tops[s] - top)
+        factor[h, :, 0:3, :] = jnp.exp(stat_send[h, :, 0:3, :] - top) / total
+        for j in range(TILES // 2):
+            here = tile(h * (TILES // 2) + j)
+            r = j % 3
+            resp[:, here] = (acc[:, here] * factor[h, j // 3, r : r + 1, :]).astype(BF16)
 
     def sums_x(p):
         both = pl.ds(pl.multiple_of(2 * W * p, 2 * W), 2 * W)
@@ -421,41 +433,32 @@
         second[p, x, HOME] = jnp.concatenate([left, right], axis=0).astype(BF16)
         spread_z(second, p, uz_send, uz_recv)
 
-    renew(0)
-    renew(1)
-    done = 1
-    for p, g in in_order(0.9):
-        if done < min(p + 1 + (GROUPS - 1 - g) // 2, PARTS - 1) or done < p:
-            done += 1
-            renew(done)
-        spread_x(second, p, g, ux_send, (uz_recv, ux_recv))
+    each_part(renew)
+    for p in range(PARTS):
+        for g in reversed(range(GROUPS)):
+            spread_x(second, p, g, ux_send, (uz_recv, ux_recv))
     pending.append(lambda: each_part(lambda p: take(second.at[p, 0, pl.ds(0, NZ - 1)], uz_send.at[p])))
     pending.append(lambda: each_part(lambda p: take(second.at[p, pl.ds(0, NX - 1)], ux_send.at[p])))
     products(second, ux_recv)
 
-    for t in range(TILES):
-        here, score = score_tile(t)
-        top = jnp.max(score, axis=0, keepdims=True)
-        shifted = score - top
-        weight = jnp.exp(shifted)
-        stat2_send[t, 0:1, :] = top
-        stat2_send[t, 1:2, :] = jnp.sum(weight, axis=0, keepdims=True)
-        stat2_send[t, 2:3, :] = jnp.sum(weight * shifted, axis=0, keepdims=True)
-
-    def chip_tiles(chip):
-        return pl.ds(chip * CHIP_TILES, CHIP_TILES)
-
-    for k in range(1, NCENT):
-        to = (cent + k) % NCENT
-        remote(
-            stat2_send.at[chip_tiles(to // NC)],
-            stat2_recv.at[cent],
-            st2_send.at[0],
-            st2_recv.at[0],
-            at_cent(to),
-        ).start()
+    for k in (2, 1, 3, 0):
+        chip = lax.rem(y + k, NY)
+        for j in range(CHIP_TILES):
+            here = pl.ds(pl.multiple_of(chip * CHIP + j * LANES, LANES), LANES)
+            score = score_at(here)
+            top = jnp.max(score, axis=0, keepdims=True)
+            shifted = score - top
+            weight = jnp.exp(shifted)
+            stat2_send[k, j, 0:1, :] = top
+            stat2_send[k, j, 1:2, :] = jnp.sum(weight, axis=0, keepdims=True)
+            stat2_send[k, j, 2:3, :] = jnp.sum(weight * shifted, axis=0, keepdims=True)
+        targets = (chip * NC + core, chip * NC + 1 - core) if k else (chip * NC + 1 - core,)
+        for to in targets:
+            remote(
+                stat2_send.at[k], stat2_recv.at[cent], st2_send.at[0], st2_recv.at[0], at_cent(to)
+            ).start()
     pending.append(lambda: take(stat2_recv.at[pl.ds(0, NCENT - 1)], st2_send.at[0]))
-    stat2_recv[cent] = stat2_send[chip_tiles(y)]
+    stat2_recv[cent] = stat2_send[0]
     finish()
     take(stat2_recv.at[pl.ds(0, NCENT - 1)], st2_recv.at[0])
     tops = [stat2_recv[s, :, 0:1, :] for s in range(NCENT)]
@@ -497,10 +500,10 @@
             vmem((1, GROUP), F32),
             vmem((SLICE, GROUP), F32),
             vmem((SLICE, GROUP), BF16),
-            vmem((3, 8, LANES), F32),
-            vmem((NCENT, 3, 8, LANES), F32),
-            vmem((3, 4, LANES), F32),
-            vmem((TILES, 8, LANES), F32),
+            vmem((2, 2, 8, LANES), F32),
+            vmem((2, NCENT, 2, 8, LANES), F32),
+            vmem((2, 2, 8, LANES), F32),
+            vmem((NY, CHIP_TILES, 8, LANES), F32),
             vmem((NCENT, CHIP_TILES, 8, LANES), F32),
             vmem(gathered, F32),
             vmem(gathered, BF16),
@@ -518,8 +521,8 @@
             dma((PARTS, GROUPS)),
             dma((PARTS,)),
             dma((PARTS,)),
-            dma((1,)),
-            dma((1,)),
+            dma((2,)),
+            dma((2,)),
             dma((PARTS,)),
             dma((PARTS, GROUPS)),
             dma((PARTS,)),

time: 95.8 us -> 92.3 us (0.963)
  Pallas kernels: 92.2 us -> 88.7 us
    pallas_call x1, Pallas kernels: 92.2 us -> 88.7 us  [on_device(): pl.pallas_call(kernel, out_shape=(jax.ShapeDtypeStruct((OWN, D), F32), ja...]
where the time goes in v4:
time: 92.3 us; the launch traced here: 92.1 us
  Pallas kernels  88.7 us (96%)
  local copies, waits for them, and re-layouts  2.66 us (3%)
    pallas_call x1, Pallas kernels, on_device(): pl.pallas_call(kernel, out_shape=(jax.ShapeDtypeStruct((OWN, D), F32), ja...  88.7 us
    unnamed x3, local copies, waits for them, and re-layouts  2.02 us

profile of v4, /device:TPU:1, one launch (start us, length us, event | category | flops | bytes accessed | tf_op | source)
XLA Modules:
  0.0 92.1 jit_solution(6354167627019846461)
XLA Ops:
  0.6 88.7 %em_update.1 = (f32[8,1024]{1,0:T(8,128)}, f32[3,1,128]{2,1,0:T(1,128)}) custom-call(f32[192,1024]{1,0:T(8,128)} %emb_hbm.1, f32[8,1024]{1,0:T(8,128)} %cent_hbm.1), custom_call_target="tpu_custom_call" | custom-call | tf_op jit(solution)/shard_map/em_update/pallas_call | solution.py:483
  89.4 0.0 copy-start
  89.4 0.6 copy-done
  90.0 0.6 dynamic_slice.3
  90.7 1.4 %copy.5 = f32[8,1024]{1,0:T(8,128)} copy(f32[8,1024]{1,0:T(8,128)} %get-tuple-element.8) | data formatting | bytes 65536
  (1 shorter events, 0.0 us)
Async XLA Ops:
  89.4 0.7 copy-start

commit v5 on v4

--- a/solution.py
+++ b/solution.py
@@ -357,12 +357,11 @@
     for t in range(TILES):
         mass_part += resp[:, t * LANES : (t + 1) * LANES].astype(F32)
     norm_part[...] = mass_part
-    lane = lax.broadcasted_iota(jnp.int32, (NZ, OWN, LANES), 2)
-    layer = lax.broadcasted_iota(jnp.int32, (NZ, OWN, LANES), 0)
+    block = (NZ * OWN, LANES)
+    diagonal = lax.broadcasted_iota(jnp.int32, block, 0) == lax.broadcasted_iota(jnp.int32, block, 1)
     for i in range(NX):
         mass = jnp.sum(norm_part[i * NZ * OWN : (i + 1) * NZ * OWN, :], axis=1, keepdims=True)
-        mass = jnp.broadcast_to(mass, (NZ * OWN, LANES)).reshape(NZ, OWN, LANES)
-        count_send[i] = jnp.sum(jnp.where(lane == layer, mass, 0.0), axis=0)
+        count_send[i] = jnp.sum(jnp.where(diagonal, mass, 0.0), axis=0, keepdims=True)
     for k in (2, 1, 3):
         to = lax.rem(x + k, NX)
         remote(
@@ -415,10 +414,11 @@
     acc[...] = jnp.zeros_like(acc)
 
     take(total_recv.at[pl.ds(0, NZ - 1)], nz_recv.at[0])
+    row = lax.broadcasted_iota(jnp.int32, (OWN, LANES), 0)
     lane = lax.broadcasted_iota(jnp.int32, (OWN, LANES), 1)
     mass = jnp.zeros((OWN, LANES), F32)
     for slot in range(NZ):
-        mass += jnp.where(lane == BACK[slot], total_recv[slot], 0.0)
+        mass += jnp.where(lane == BACK[slot] * OWN + row, total_recv[slot], 0.0)
     mass = jnp.sum(mass, axis=1, keepdims=True) + prior_mass
 
     def renew(p):
@@ -510,10 +510,10 @@
             vmem(gathered, BF16),
             vmem((PARTS, NZ, 2 * OWN, W), BF16),
             vmem((PARTS, NZ, 2 * OWN, W), BF16),
-            vmem((NX, OWN, LANES), F32),
-            vmem((NX, OWN, LANES), F32),
-            vmem((OWN, LANES), F32),
-            vmem((NZ, OWN, LANES), F32),
+            vmem((NX, 1, LANES), F32),
+            vmem((NX, 1, LANES), F32),
+            vmem((1, LANES), F32),
+            vmem((NZ, 1, LANES), F32),
             dma((2,)),
             dma((14,)),
             dma((NCENT, 2)),

time: 92.3 us -> 89.9 us (0.974)
  Pallas kernels: 88.7 us -> 86.4 us
    pallas_call x1, Pallas kernels: 88.7 us -> 86.4 us  [on_device(): pl.pallas_call(kernel, out_shape=(jax.ShapeDtypeStruct((OWN, D), F32), ja...]
where the time goes in v5:
time: 89.9 us; the launch traced here: 89.7 us
  Pallas kernels  86.4 us (96%)
  local copies, waits for them, and re-layouts  2.66 us (3%)
    pallas_call x1, Pallas kernels, on_device(): pl.pallas_call(kernel, out_shape=(jax.ShapeDtypeStruct((OWN, D), F32), ja...  86.4 us
    unnamed x3, local copies, waits for them, and re-layouts  2.02 us

profile of v5, /device:TPU:1, one launch (start us, length us, event | category | flops | bytes accessed | tf_op | source)
XLA Modules:
  0.0 89.7 jit_solution(2575763816837802260)
XLA Ops:
  0.6 86.4 %em_update.1 = (f32[8,1024]{1,0:T(8,128)}, f32[3,1,128]{2,1,0:T(1,128)}) custom-call(f32[192,1024]{1,0:T(8,128)} %emb_hbm.1, f32[8,1024]{1,0:T(8,128)} %cent_hbm.1), custom_call_target="tpu_custom_call" | custom-call | tf_op jit(solution)/shard_map/em_update/pallas_call | solution.py:483
  87.0 0.0 copy-start
  87.0 0.6 copy-done
  87.7 0.6 dynamic_slice.3
  88.3 1.4 %copy.5 = f32[8,1024]{1,0:T(8,128)} copy(f32[8,1024]{1,0:T(8,128)} %get-tuple-element.8) | data formatting | bytes 65536
  (1 shorter events, 0.0 us)
Async XLA Ops:
  87.0 0.7 copy-start

commit v6 on v5

--- a/solution.py
+++ b/solution.py
@@ -31,6 +31,8 @@
 BACK = tuple(SLOT[(NZ - offset) % NZ] for offset in OFFSETS)
 GROUPS = 4
 PER = NZ // GROUPS
+SUM_GROUPS = 8
+SUM_PER = NZ // SUM_GROUPS
 HOME = NZ - 1
 HALF = ROWS // 2
 
@@ -339,8 +341,8 @@
             packed = jnp.concatenate([left, right], axis=1)
             sums_f[p, i] = packed
             sums_send[p, i] = packed.astype(BF16)
-        for g in range(GROUPS):
-            group = pl.ds(g * PER, PER)
+        for g in range(SUM_GROUPS):
+            group = pl.ds(g * SUM_PER, SUM_PER)
             for k in (2, 1, 3):
                 to = lax.rem(x + k, NX)
                 remote(
@@ -374,14 +376,14 @@
     pending.append(lambda: each_part(lambda p: take(sums_recv.at[p, pl.ds(0, NX - 1)], cx_send.at[p])))
 
     def sums_z(p):
-        for g in range(GROUPS):
-            group = slice(g * PER, (g + 1) * PER)
-            take(sums_recv.at[p, pl.ds(0, NX - 1), pl.ds(g * PER, PER)], cx_recv.at[p, g])
+        for g in range(SUM_GROUPS):
+            group = slice(g * SUM_PER, (g + 1) * SUM_PER)
+            take(sums_recv.at[p, pl.ds(0, NX - 1), pl.ds(g * SUM_PER, SUM_PER)], cx_recv.at[p, g])
             value = sums_f[p, x, group]
             for k in range(1, NX):
                 value += sums_recv[p, lax.rem(x + k, NX), group].astype(F32)
             part_send[p, group] = value.astype(BF16)
-            for slot in range(g * PER, (g + 1) * PER):
+            for slot in range(g * SUM_PER, (g + 1) * SUM_PER):
                 if slot != HOME:
                     remote(
                         part_send.at[p, slot],
@@ -524,7 +526,7 @@
             dma((2,)),
             dma((2,)),
             dma((PARTS,)),
-            dma((PARTS, GROUPS)),
+            dma((PARTS, SUM_GROUPS)),
             dma((PARTS,)),
             dma((PARTS,)),
             dma((1,)),

time: 89.9 us -> 89.5 us (level)
  no operation moved by 1% of the time
where the time goes in v6:
time: 89.5 us; the launch traced here: 89.3 us
  Pallas kernels  86 us (96%)
  local copies, waits for them, and re-layouts  2.66 us (3%)
    pallas_call x1, Pallas kernels, on_device(): pl.pallas_call(kernel, out_shape=(jax.ShapeDtypeStruct((OWN, D), F32), ja...  86 us
    unnamed x3, local copies, waits for them, and re-layouts  2.02 us

profile of v6, /device:TPU:1, one launch (start us, length us, event | category | flops | bytes accessed | tf_op | source)
XLA Modules:
  0.0 89.3 jit_solution(13588921948798585493)
XLA Ops:
  0.6 86.0 %em_update.1 = (f32[8,1024]{1,0:T(8,128)}, f32[3,1,128]{2,1,0:T(1,128)}) custom-call(f32[192,1024]{1,0:T(8,128)} %emb_hbm.1, f32[8,1024]{1,0:T(8,128)} %cent_hbm.1), custom_call_target="tpu_custom_call" | custom-call | tf_op jit(solution)/shard_map/em_update/pallas_call | solution.py:485
  86.6 0.0 copy-start
  86.6 0.6 copy-done
  87.3 0.6 dynamic_slice.3
  87.9 1.4 %copy.5 = f32[8,1024]{1,0:T(8,128)} copy(f32[8,1024]{1,0:T(8,128)} %get-tuple-element.8) | data formatting | bytes 65536
  (1 shorter events, 0.0 us)
Async XLA Ops:
  86.6 0.7 copy-start
